TPU v7x, 32 devices: a whole 2x2x4 slice. The times are simulated.
32 devices in a mesh: groups: 2 (over x), blk: 16 (over z, y, core).
Axes of the slice: x: 2, y: 2, z: 4, core: 2. Of those that a mesh axis runs over, the one named last changes fastest.
Arguments:
- queries: bfloat16 [4096, 512], P(('groups', 'blk')), parts along dimension 0, may hold values from -8 to 8
- key_states: bfloat16 [4096, 128], P(('groups', 'blk')), parts along dimension 0, may hold values from -6 to 6
- value_states: bfloat16 [4096, 128], P(('groups', 'blk')), parts along dimension 0, may hold values from -6 to 6
- grad_out: bfloat16 [4096, 512], P(('groups', 'blk')), parts along dimension 0, may hold values from -6 to 6
- tile_mask: int32 [32, 16], P('groups'), parts along dimension 0, may hold values 0 or 1
- block_order: int32 [32], P('groups'), parts along dimension 0, may hold values from 0 to 15, each once
Outputs:
- attended: bfloat16 [4096, 512], P(('groups', 'blk')), parts along dimension 0
- grad_queries: bfloat16 [4096, 512], P(('groups', 'blk')), parts along dimension 0
- grad_keys: float32 [4096, 128], P(('groups', 'blk')), parts along dimension 0
- grad_values: float32 [4096, 128], P(('groups', 'blk')), parts along dimension 0
There are 2 independent parts, one for each index of `groups`. A program takes and returns all parts, laid end to end along the dimension named above; each array names one. Nothing has to cross between parts.
Inputs may be any that keep to these rules, and one draw needn't show every extreme that they name: `block_order`: each block number appears once.
All inputs are finite; a program needn't handle non-finite values.
Results may differ from a plain program's by a relative error of at most 0.04.
Values may be sent and summed in bfloat16 or wider, within the bound.
A program may use at most 64 MiB of HBM per device.

v0:
```python
import functools
import math

import jax
import jax.numpy as jnp
from jax import lax
from jax.experimental import pallas as pl
from jax.experimental.pallas import tpu as pltpu
from jax.sharding import PartitionSpec as P

MESH = pl.DeviceIdType.MESH
F32 = jnp.float32
BF16 = jnp.bfloat16
MASKED = -1e30


def dot(a, b):
    return jnp.dot(a, b, preferred_element_type=F32)


def kernel(
    n, q_hbm, k_hbm, v_hbm, g_hbm, mask_hbm, order_hbm, att_ref, dq_ref, dk_ref, dv_ref,
    mask_ref, order_ref, q_ref, g_ref, kv, qr, qt, gr, gt, prob, dprob, maxes, acc, send_a, recv_a, send_b, recv_b, send_c, recv_c,
    in_s, gz_s, gz_r, gy_s, gy_r, gc_s, gc_r, a_s, a_r, b_s, b_r, c_s, c_r,
):
    m = n // 4
    tok, hd = k_hbm.shape
    heads = q_hbm.shape[1] // hd
    rows = heads * tok
    scale = hd ** -0.5
    to_exp2 = scale * math.log2(math.e)
    KEY, VALUE = 0, 1

    me = lax.axis_index("blk")
    z, y, c = me // 4, (me // 2) % 2, me % 2

    def index(rz, ry, rc):
        zz = lax.rem(z + rz, m)
        yy = 1 - y if ry else y
        cc = 1 - c if rc else c
        return (zz * 2 + yy) * 2 + cc

    def remote(src, dst, s_sem, r_sem, target):
        return pltpu.make_async_remote_copy(
            src_ref=src, dst_ref=dst, send_sem=s_sem, recv_sem=r_sem,
            device_id={"blk": target}, device_id_type=MESH,
        )

    partner, sibling = index(0, 1, 1), index(0, 0, 1)

    def side(rz, ry):
        return (1 if rz else 0) ^ ry

    def gather_z(t, g):
        return remote(
            kv.at[t, 0, 0, 0], kv.at[t, m - g, 1, 0], gz_s.at[t, g], gz_r.at[t, m - g], index(g, 0, 1)
        )

    def gather_y(t, rz):
        return remote(
            kv.at[t, rz, side(rz, 0), 0], kv.at[t, rz, side(rz, 1), 1], gy_s.at[t, rz], gy_r.at[t, rz], partner
        )

    def gather_c(t, rz, ry):
        near = side(rz, ry)
        return remote(
            kv.at[t, rz, near, ry], kv.at[t, rz, 1 - near, ry], gc_s.at[t, rz, ry], gc_r.at[t, rz, ry], sibling
        )

    def sum_a(t, rz):
        return remote(send_a.at[t, rz], recv_a.at[t, rz], a_s.at[t, rz], a_r.at[t, rz], sibling)

    def sum_b(t, rz):
        return remote(send_b.at[t, rz], recv_b.at[t, rz], b_s.at[t, rz], b_r.at[t, rz], partner)

    def sum_c(t, rz):
        return remote(send_c.at[t, rz], recv_c.at[t, rz], c_s.at[t, rz], c_r.at[t, rz], index(rz, 0, 1))

    barrier = pltpu.get_barrier_semaphore()
    for other in [index(g, 0, 1) for g in range(1, m)] + [partner, sibling]:
        pl.semaphore_signal(barrier, inc=1, device_id={"blk": other}, device_id_type=MESH)
    loads = [
        pltpu.make_async_copy(src, dst, in_s.at[i])
        for i, (src, dst) in enumerate(
            [(k_hbm, kv.at[KEY, 0, 0, 0]), (v_hbm, kv.at[VALUE, 0, 0, 0]), (q_hbm, q_ref), (g_hbm, g_ref),
             (mask_hbm, mask_ref), (order_hbm, order_ref)]
        )
    ]
    for load in loads:
        load.start()
    for load in loads:
        load.wait()
    pl.semaphore_wait(barrier, m + 1)

    order = sorted(range(1, m), key=lambda r: min(r, m - r))
    steps = [0] + order
    back = order[::-1] + [0]
    for t in (KEY, VALUE):
        gather_y(t, 0).start()
        for rz in order:
            gather_z(t, m - rz).start()
        gather_c(t, 0, 0).start()

    for h in range(heads):
        cols = slice(h * hd, (h + 1) * hd)
        lanes = slice(h * tok, (h + 1) * tok)
        qr[lanes, :] = q_ref[:, cols]
        gr[lanes, :] = g_ref[:, cols]
        qt[:, lanes] = q_ref[:, cols].T
        gt[:, lanes] = g_ref[:, cols].T

    my_block = order_ref[me]
    key_ids = lax.broadcasted_iota(jnp.int32, (tok, rows), 0)
    row_ids = lax.broadcasted_iota(jnp.int32, (tok, rows), 1) % tok
    causal = jnp.where(row_ids >= key_ids, 0.0, MASKED).astype(F32)

    def bias(rz, rc, ry):
        if rz == 0 and rc == 0 and ry == 0:
            return causal
        block = order_ref[index(rz, ry, rc)]
        seen = (my_block > block) & (mask_ref[my_block, block] == 1)
        return jnp.where(seen, 0.0, MASKED).astype(F32)

    parts = [(rc, ry) for rc in range(2) for ry in range(2)]

    def pump_y(t, rz):
        gather_y(t, rz).wait_recv()
        gather_c(t, rz, 1).start()

    def pump_z(t, rz):
        gather_z(t, m - rz).wait_recv()
        gather_y(t, rz).start()
        gather_c(t, rz, 0).start()

    def landed(t, rz):
        gather_c(t, rz, 0).wait_recv()
        gather_c(t, rz, 1).wait_recv()
        return kv[t, rz].reshape(4 * tok, hd)

    def score(rz, run_max, run_sum):
        scores = dot(landed(KEY, rz), qt[...])
        scores = [
            scores[i * tok:(i + 1) * tok] * to_exp2 + bias(rz, rc, ry)
            for i, (rc, ry) in enumerate(parts)
        ]
        new_max = run_max
        for s in scores:
            new_max = jnp.maximum(new_max, jnp.max(s, axis=0, keepdims=True))
        run_sum = run_sum * jnp.exp2(run_max - new_max)
        for i, s in enumerate(scores):
            p = jnp.exp2(s - new_max)
            run_sum = run_sum + jnp.sum(p, axis=0, keepdims=True)
            prob[rz, i * tok:(i + 1) * tok, :] = p.astype(BF16)
        maxes[rz] = new_max
        return new_max, run_sum

    for rz in order:
        pump_z(KEY, rz)
    pump_y(KEY, 0)
    run_max = jnp.full((1, rows), MASKED, F32)
    run_sum = jnp.zeros((1, rows), F32)
    run_max, run_sum = score(0, run_max, run_sum)
    for rz in order:
        pump_y(KEY, rz)
        pump_z(VALUE, rz)
    pump_y(VALUE, 0)
    for rz in order:
        run_max, run_sum = score(rz, run_max, run_sum)
    inverse = 1.0 / run_sum

    def hand_over(t, rz, grad):
        for i, (rc, ry) in enumerate(parts):
            part = slice(i * tok, (i + 1) * tok)
            if rc != side(rz, ry):
                send_a[t, rz, ry] = grad[part].astype(BF16)
            else:
                acc[t, rz, ry] = grad[part]
        sum_a(t, rz).start()

    def value_grad(rz):
        factor = jnp.exp2(maxes[rz] - run_max) * inverse
        for i in range(4):
            part = slice(i * tok, (i + 1) * tok)
            prob[rz, part, :] = (prob[rz, part, :].astype(F32) * factor).astype(BF16)
        hand_over(VALUE, rz, dot(prob[rz], gr[...]))

    def key_grad(rz, delta):
        for i in range(4):
            part = slice(i * tok, (i + 1) * tok)
            ds = prob[rz, part, :].astype(F32) * (dprob[rz, part, :] - delta)
            prob[rz, part, :] = ds.astype(BF16)
        hand_over(KEY, rz, dot(prob[rz], qr[...]))

    def level_b(t, rz):
        sum_a(t, rz).wait_recv()
        send_b[t, rz] = (acc[t, rz, 1] + recv_a[t, rz, 1].astype(F32)).astype(BF16)
        sum_b(t, rz).start()

    def level_c(t, rz):
        sum_b(t, rz).wait_recv()
        total = acc[t, rz, 0] + recv_a[t, rz, 0].astype(F32) + recv_b[t, rz].astype(F32)
        if rz == 0:
            acc[t, 0, 0] = total
        else:
            send_c[t, rz] = total.astype(BF16)
            sum_c(t, rz).start()

    for step in range(m + 1):
        if step < m:
            value_grad(back[step])
        if step:
            level_b(VALUE, back[step - 1])
    for rz in order:
        pump_y(VALUE, rz)
    out_t = jnp.zeros((hd, rows), F32)
    for step, rz in enumerate(steps):
        values = landed(VALUE, rz)
        dprob[rz] = dot(values, gt[...])
        out_t = out_t + dot(values.T, prob[rz])
        level_c(VALUE, back[step])
    out_t = out_t.astype(BF16)
    delta = jnp.sum(gt[...].astype(F32) * out_t.astype(F32), axis=0, keepdims=True)

    for step in range(m + 1):
        if step < m:
            key_grad(back[step], delta)
        if step:
            level_b(KEY, back[step - 1])

    for rz in back:
        level_c(KEY, rz)

    dq_t = jnp.zeros((hd, rows), F32)
    for rz in range(m):
        dq_t = dq_t + dot(kv[KEY, rz].reshape(4 * tok, hd).T, prob[rz])
    dq_t = (dq_t * scale).astype(BF16)
    for h in range(heads):
        cols = slice(h * hd, (h + 1) * hd)
        lanes = slice(h * tok, (h + 1) * tok)
        att_ref[:, cols] = out_t[:, lanes].T
        dq_ref[:, cols] = dq_t[:, lanes].T

    for t, out_ref, by in ((VALUE, dv_ref, 1.0), (KEY, dk_ref, scale)):
        total = acc[t, 0, 0]
        for rz in back[:-1]:
            sum_c(t, rz).wait_recv()
            total = total + recv_c[t, rz].astype(F32)
        out_ref[...] = total * by

    for t in (KEY, VALUE):
        for rz in range(m):
            gather_y(t, rz).wait_send()
            gather_c(t, rz, 0).wait_send()
            gather_c(t, rz, 1).wait_send()
            sum_a(t, rz).wait_send()
            sum_b(t, rz).wait_send()
            if rz:
                gather_z(t, rz).wait_send()
                sum_c(t, rz).wait_send()


def write_out(*refs):
    out_s = refs[8]
    stores = [pltpu.make_async_copy(refs[i], refs[4 + i], out_s.at[i]) for i in range(4)]
    for store in stores:
        store.start()
    for store in stores:
        store.wait()


def shards(queries, key_states, value_states, grad_out, tile_mask, block_order):
    n = lax.axis_size("blk")
    m = n // 4
    tok, hd = key_states.shape
    rows = queries.shape[1] // hd * tok
    assert n == 4 * m and tile_mask.shape[1] == n
    hbm = pl.BlockSpec(memory_space=pltpu.HBM)
    vmem = pl.BlockSpec(memory_space=pltpu.VMEM)
    dma = pltpu.SemaphoreType.DMA
    shapes = (
        jax.ShapeDtypeStruct(queries.shape, BF16),
        jax.ShapeDtypeStruct(queries.shape, BF16),
        jax.ShapeDtypeStruct(key_states.shape, F32),
        jax.ShapeDtypeStruct(key_states.shape, F32),
    )
    results = pl.pallas_call(
        functools.partial(kernel, n),
        out_shape=tuple(pltpu.VMEM(s.shape, s.dtype) for s in shapes),
        in_specs=[hbm] * 6,
        out_specs=(vmem,) * 4,
        scratch_shapes=[
            pltpu.SMEM(tile_mask.shape, jnp.int32),
            pltpu.SMEM(block_order.shape, jnp.int32),
            pltpu.VMEM(queries.shape, BF16),
            pltpu.VMEM(queries.shape, BF16),
            pltpu.VMEM((2, m, 2, 2, tok, hd), BF16),
            pltpu.VMEM((rows, hd), BF16),
            pltpu.VMEM((hd, rows), BF16),
            pltpu.VMEM((rows, hd), BF16),
            pltpu.VMEM((hd, rows), BF16),
            pltpu.VMEM((m, 4 * tok, rows), BF16),
            pltpu.VMEM((m, 4 * tok, rows), F32),
            pltpu.VMEM((m, 1, rows), F32),
            pltpu.VMEM((2, m, 2, tok, hd), F32),
            pltpu.VMEM((2, m, 2, tok, hd), BF16),
            pltpu.VMEM((2, m, 2, tok, hd), BF16),
            pltpu.VMEM((2, m, tok, hd), BF16),
            pltpu.VMEM((2, m, tok, hd), BF16),
            pltpu.VMEM((2, m, tok, hd), BF16),
            pltpu.VMEM((2, m, tok, hd), BF16),
            dma((6,)), dma((2, m)), dma((2, m)), dma((2, m)), dma((2, m)), dma((2, m, 2)), dma((2, m, 2)),
            dma((2, m)), dma((2, m)), dma((2, m)), dma((2, m)), dma((2, m)), dma((2, m)),
        ],
        compiler_params=pltpu.CompilerParams(
            collective_id=0, has_side_effects=True, vmem_limit_bytes=58 * 1024 * 1024
        ),
    )(queries, key_states, value_states, grad_out, tile_mask, block_order)
    return pl.pallas_call(
        write_out,
        out_shape=shapes,
        in_specs=[vmem] * 4,
        out_specs=(hbm,) * 4,
        scratch_shapes=[dma((4,))],
        compiler_params=pltpu.CompilerParams(vmem_limit_bytes=8 * 1024 * 1024),
    )(*results)


def solution(mesh):
    both = P(("groups", "blk"), None)
    return jax.shard_map(
        shards,
        mesh=mesh,
        in_specs=(both, both, both, both, P("groups", None), P("groups")),
        out_specs=(both, both, both, both),
        check_vma=False,
    )
```

profile of v0, /device:TPU:0, one launch (start us, length us, event | category | flops | bytes accessed | tf_op | source)
XLA Modules:
  0.0 32.6 jit_solution(3699870186294157849)
XLA Ops:
  0.6 31.2 %shard_map.93 = (bf16[128,512]{1,0:T(8,128)(2,1)S(1)}, bf16[128,512]{1,0:T(8,128)(2,1)S(1)}, f32[128,128]{1,0:T(8,128)S(1)}, f32[128,128]{1,0:T(8,128)S(1)}) custom-call(bf16[128,512]{1,0:T(8,128)(2,1)} %q_hbm.1, bf16[128,128]{1,0:T(8,128)(2,1)} %k_hbm.1, bf16[128,128]{1,0:T(8,128)(2,1)} %v_hbm.1, bf16[128,512]{1,0:T(8,128)(2,1)} %g_hbm.1, ...), custom_call_target="tpu_custom_call" | custom-call | tf_op jit(solution)/shard_map/pallas_call | solution.py:286
  31.8 0.8 %shard_map.94 = (bf16[128,512]{1,0:T(8,128)(2,1)}, bf16[128,512]{1,0:T(8,128)(2,1)}, f32[128,128]{1,0:T(8,128)}, f32[128,128]{1,0:T(8,128)}) custom-call(bf16[128,512]{1,0:T(8,128)(2,1)S(1)} %get-tuple-element.8.refs_0_, bf16[128,512]{1,0:T(8,128)(2,1)S(1)} %get-tuple-element.9.refs_1_, f32[128,128]{1,0:T(8,128)S(1)} %get-tuple-element.10.refs_2_, ...), custom_call_target="tpu_custom_call" | custom-call | tf_op jit(solution)/shard_map/pallas_call | solution.py:318
where the time goes:
time: 32.7 us; the launch traced here: 32.6 us
  Pallas kernels  32 us (98%)
  between operations  0.64 us (2%)
    pallas_call x1, Pallas kernels, shards(): pl.pallas_call(functools.partial(kernel, n), out_shape=tuple((pltpu.VMEM(...  31.2 us
    pallas_call x1, Pallas kernels, shards(): pl.pallas_call(write_out, out_shape=shapes, in_specs=[vmem] * 4, out_spec...  0.77 us

commit v1 on v0

v1 whole, which is shorter than its diff:
```python
import functools
import math

import jax
import jax.numpy as jnp
from jax import lax
from jax.experimental import pallas as pl
from jax.experimental.pallas import tpu as pltpu
from jax.sharding import PartitionSpec as P

MESH = pl.DeviceIdType.MESH
F32 = jnp.float32
BF16 = jnp.bfloat16
MASKED = -1e30


def dot(a, b):
    return jnp.dot(a, b, preferred_element_type=F32)


def dot_t(a, b):
    return lax.dot_general(a, b, (((1,), (1,)), ((), ())), preferred_element_type=F32)


def kernel(
    n, q_hbm, k_hbm, v_hbm, g_hbm, mask_hbm, order_hbm, att_ref, dq_ref, dk_ref, dv_ref,
    mask_ref, order_ref, q_ref, g_ref, kv, rt, prob, dprob, stat, mine, send_z, recv_z, send_c, recv_c, send_y, recv_y,
    in_s, z_s, z_r, y_s, y_r, c_s, c_r, f_s, f_r, t_s, t_r, gz_s, gz_r, gc_s, gc_r, gy_s, gy_r,
):
    m = n // 4
    tok, hd = k_hbm.shape
    heads = q_hbm.shape[1] // hd
    rows = heads * tok
    keys = m * tok
    scale = hd ** -0.5
    to_exp2 = scale * math.log2(math.e)
    KEY, VALUE = 0, 1
    QUERY, GRAD = 0, 1
    OUT, DQ = 0, 1
    OWN, SIBLING, DIAGONAL, PARTNER = 0, 1, 2, 3
    quad = (OWN, SIBLING, DIAGONAL, PARTNER)
    others = (DIAGONAL, PARTNER, SIBLING)

    me = lax.axis_index("blk")
    z, y, c = me // 4, (me // 2) % 2, me % 2

    def index(rz, j):
        zz = lax.rem(z + rz, m)
        yy = 1 - y if j & 2 else y
        cc = 1 - c if j & 1 else c
        return (zz * 2 + yy) * 2 + cc

    def chunk(rz):
        return index(rz, 1 if rz else 0)

    def remote(src, dst, s_sem, r_sem, target):
        return pltpu.make_async_remote_copy(
            src_ref=src, dst_ref=dst, send_sem=s_sem, recv_sem=r_sem,
            device_id={"blk": target}, device_id_type=MESH,
        )

    def gather_z(t, g):
        return remote(kv.at[t, 0], kv.at[t, m - g], z_s.at[t, g], z_r.at[t, m - g], chunk(g))

    def gather_y(t):
        return remote(rt.at[t, OWN], rt.at[t, PARTNER], y_s.at[t], y_r.at[t], index(0, PARTNER))

    def gather_c(t):
        return remote(rt.at[t, OWN], rt.at[t, SIBLING], c_s.at[t], c_r.at[t], index(0, SIBLING))

    def forward(t):
        return remote(rt.at[t, PARTNER], rt.at[t, DIAGONAL], f_s.at[t], f_r.at[t], index(0, SIBLING))

    def share(t, j):
        return remote(stat.at[t, OWN], stat.at[t, j], t_s.at[t, j], t_r.at[t, j], index(0, j))

    def sum_z(t, rz):
        return remote(send_z.at[t, rz], recv_z.at[t, m - rz], gz_s.at[t, rz], gz_r.at[t, m - rz], chunk(rz))

    def sum_c(t, i):
        return remote(send_c.at[t, i], recv_c.at[t, i], gc_s.at[t, i], gc_r.at[t, i], index(0, SIBLING))

    def sum_y(t):
        return remote(send_y.at[t], recv_y.at[t], gy_s.at[t], gy_r.at[t], index(0, PARTNER))

    barrier = pltpu.get_barrier_semaphore()
    for other in [chunk(g) for g in range(1, m)] + [index(0, j) for j in others]:
        pl.semaphore_signal(barrier, inc=1, device_id={"blk": other}, device_id_type=MESH)
    loads = [
        pltpu.make_async_copy(src, dst, in_s.at[i])
        for i, (src, dst) in enumerate(
            [(q_hbm, q_ref), (g_hbm, g_ref), (k_hbm, kv.at[KEY, 0]), (v_hbm, kv.at[VALUE, 0]),
             (mask_hbm, mask_ref), (order_hbm, order_ref)]
        )
    ]
    for load in loads:
        load.start()
    for t, ref in ((QUERY, q_ref), (GRAD, g_ref)):
        loads[t].wait()
        for h in range(heads):
            rt[t, OWN, :, h * tok:(h + 1) * tok] = ref[:, h * hd:(h + 1) * hd].T
    for load in loads[2:]:
        load.wait()
    pl.semaphore_wait(barrier, m + 2)

    far = sorted(range(1, m), key=lambda r: -min(r, m - r))
    for t in (0, 1):
        for rz in far:
            gather_z(t, rz).start()
        gather_y(t).start()
        gather_c(t).start()

    blocks = [order_ref[index(0, j)] for j in quad]
    key_ids = lax.broadcasted_iota(jnp.int32, (tok, rows), 0)
    row_ids = lax.broadcasted_iota(jnp.int32, (tok, rows), 1) % tok
    causal = jnp.where(row_ids >= key_ids, 0.0, MASKED).astype(F32)

    def bias(j, rz):
        if rz == 0 and j == OWN:
            return causal
        block = order_ref[chunk(rz)]
        seen = (blocks[j] > block) & (mask_ref[blocks[j], block] == 1)
        return jnp.where(seen, 0.0, MASKED).astype(F32)

    def flat(t):
        return kv[t].reshape(keys, hd)

    def score(j):
        scores = dot(flat(KEY), rt[QUERY, j])
        top = jnp.full((1, rows), 0.1 * MASKED, F32)
        parts = []
        for rz in range(m):
            s = scores[rz * tok:(rz + 1) * tok]
            b = bias(j, rz)
            if rz == 0 and j == OWN:
                s = s * to_exp2 + b
                top = jnp.maximum(top, jnp.max(s, axis=0, keepdims=True))
            else:
                top = jnp.maximum(top, jnp.max(s, axis=0, keepdims=True) * to_exp2 + b)
            parts.append((s, b))
        total = jnp.zeros((1, rows), F32)
        for rz, (s, b) in enumerate(parts):
            if rz == 0 and j == OWN:
                p = jnp.exp2(s - top)
            else:
                p = jnp.exp2(s * to_exp2 + (b - top))
            total = total + jnp.sum(p, axis=0, keepdims=True)
            prob[j, rz * tok:(rz + 1) * tok, :] = p.astype(BF16)
        mine[0, j] = top
        stat[0, OWN, :, j * rows:(j + 1) * rows] = top + jnp.log2(jnp.maximum(total, 1e-37))

    gather_y(QUERY).wait_recv()
    forward(QUERY).start()
    for rz in range(1, m):
        gather_z(KEY, rz).wait_recv()
    score(OWN)
    gather_c(QUERY).wait_recv()
    score(SIBLING)
    score(PARTNER)
    forward(QUERY).wait_recv()
    score(DIAGONAL)
    for j in others:
        share(0, j).start()

    def prob_grad(j):
        total = jnp.zeros((1, rows), F32)
        grads = dot(flat(VALUE), rt[GRAD, j])
        dprob[j] = grads
        mine[1, j] = jnp.sum(prob[j].astype(F32) * grads, axis=0, keepdims=True)

    gather_y(GRAD).wait_recv()
    forward(GRAD).start()
    for rz in range(1, m):
        gather_z(VALUE, rz).wait_recv()
    prob_grad(OWN)
    gather_c(GRAD).wait_recv()
    prob_grad(SIBLING)
    prob_grad(PARTNER)
    forward(GRAD).wait_recv()
    prob_grad(DIAGONAL)

    def shared(t, r, j):
        return stat[t, r, :, (r ^ j) * rows:((r ^ j) + 1) * rows]

    for j in others:
        share(0, j).wait_recv()
    factors = []
    for j in quad:
        parts = [shared(0, r, j) for r in quad]
        top = jnp.maximum(jnp.maximum(parts[0], parts[1]), jnp.maximum(parts[2], parts[3]))
        total = sum(jnp.exp2(part - top) for part in parts)
        factor = jnp.exp2(mine[0, j] - top - jnp.log2(total))
        factors.append(factor)
        stat[1, OWN, :, j * rows:(j + 1) * rows] = mine[1, j] * factor
    for j in others:
        share(1, j).start()

    def key_side(t):
        total = jnp.zeros((keys, hd), F32)
        for j in quad:
            scaled = (rt[t, j].astype(F32) * factors[j]).astype(BF16)
            total = total + dot_t(prob[j], scaled)
        return total

    def send_key_side(t, total):
        for rz in far:
            send_z[t, rz] = total[rz * tok:(rz + 1) * tok].astype(BF16)
            sum_z(t, rz).start()
        return total[:tok]

    def query_side(t, left, j, by):
        return dot(left, prob[j]) * (factors[j] * by)

    def start_query_side(t, left, by):
        send_c[t, 0] = query_side(t, left, DIAGONAL, by).astype(BF16)
        sum_c(t, 0).start()
        return query_side(t, left, PARTNER, by)

    def end_query_side(t, left, by, part):
        sum_c(t, 0).wait_recv()
        send_y[t] = (part + recv_c[t, 0].astype(F32)).astype(BF16)
        sum_y(t).start()
        send_c[t, 1] = query_side(t, left, SIBLING, by).astype(BF16)
        sum_c(t, 1).start()
        return query_side(t, left, OWN, by)

    def finish_query_side(t, total, out_ref):
        sum_c(t, 1).wait_recv()
        total = total + recv_c[t, 1].astype(F32)
        sum_y(t).wait_recv()
        total = (total + recv_y[t].astype(F32)).astype(BF16)
        for h in range(heads):
            out_ref[:, h * hd:(h + 1) * hd] = total[:, h * tok:(h + 1) * tok].T

    def finish_key_side(t, total, out_ref, by):
        for rz in reversed(far):
            sum_z(t, rz).wait_recv()
            total = total + recv_z[t, m - rz].astype(F32)
        out_ref[...] = total * by

    dv = send_key_side(VALUE, key_side(VALUE))
    values_t = flat(VALUE).T
    out_part = start_query_side(OUT, values_t, 1.0)
    out = end_query_side(OUT, values_t, 1.0, out_part)

    for j in others:
        share(1, j).wait_recv()
    for j in (DIAGONAL, PARTNER, SIBLING, OWN):
        delta = sum(shared(1, r, j) for r in quad)
        prob[j] = (prob[j].astype(F32) * (dprob[j] - delta)).astype(BF16)
    keys_t = flat(KEY).T
    dq_part = start_query_side(DQ, keys_t, scale)
    dk = send_key_side(KEY, key_side(KEY))
    dq = end_query_side(DQ, keys_t, scale, dq_part)

    finish_query_side(OUT, out, att_ref)
    finish_key_side(VALUE, dv, dv_ref, 1.0)
    finish_key_side(KEY, dk, dk_ref, scale)
    finish_query_side(DQ, dq, dq_ref)

    for t in (0, 1):
        gather_y(t).wait_send()
        gather_c(t).wait_send()
        forward(t).wait_send()
        sum_y(t).wait_send()
        for i in (0, 1):
            sum_c(t, i).wait_send()
        for j in others:
            share(t, j).wait_send()
        for rz in range(1, m):
            gather_z(t, rz).wait_send()
            sum_z(t, rz).wait_send()


def write_out(*refs):
    out_s = refs[8]
    stores = [pltpu.make_async_copy(refs[i], refs[4 + i], out_s.at[i]) for i in range(4)]
    for store in stores:
        store.start()
    for store in stores:
        store.wait()


def shards(queries, key_states, value_states, grad_out, tile_mask, block_order):
    n = lax.axis_size("blk")
    m = n // 4
    tok, hd = key_states.shape
    rows = queries.shape[1] // hd * tok
    assert n == 4 * m and tile_mask.shape[1] == n
    hbm = pl.BlockSpec(memory_space=pltpu.HBM)
    vmem = pl.BlockSpec(memory_space=pltpu.VMEM)
    dma = pltpu.SemaphoreType.DMA
    shapes = (
        jax.ShapeDtypeStruct(queries.shape, BF16),
        jax.ShapeDtypeStruct(queries.shape, BF16),
        jax.ShapeDtypeStruct(key_states.shape, F32),
        jax.ShapeDtypeStruct(key_states.shape, F32),
    )
    results = pl.pallas_call(
        functools.partial(kernel, n),
        out_shape=tuple(pltpu.VMEM(s.shape, s.dtype) for s in shapes),
        in_specs=[hbm] * 6,
        out_specs=(vmem,) * 4,
        scratch_shapes=[
            pltpu.SMEM(tile_mask.shape, jnp.int32),
            pltpu.SMEM(block_order.shape, jnp.int32),
            pltpu.VMEM(queries.shape, BF16),
            pltpu.VMEM(queries.shape, BF16),
            pltpu.VMEM((2, m, tok, hd), BF16),
            pltpu.VMEM((2, 4, hd, rows), BF16),
            pltpu.VMEM((4, m * tok, rows), BF16),
            pltpu.VMEM((4, m * tok, rows), F32),
            pltpu.VMEM((2, 4, 1, 4 * rows), F32),
            pltpu.VMEM((2, 4, 1, rows), F32),
            pltpu.VMEM((2, m, tok, hd), BF16),
            pltpu.VMEM((2, m, tok, hd), BF16),
            pltpu.VMEM((2, 2, hd, rows), BF16),
            pltpu.VMEM((2, 2, hd, rows), BF16),
            pltpu.VMEM((2, hd, rows), BF16),
            pltpu.VMEM((2, hd, rows), BF16),
            dma((6,)), dma((2, m)), dma((2, m)), dma((2,)), dma((2,)), dma((2,)), dma((2,)), dma((2,)), dma((2,)),
            dma((2, 4)), dma((2, 4)), dma((2, m)), dma((2, m)), dma((2, 2)), dma((2, 2)), dma((2,)), dma((2,)),
        ],
        compiler_params=pltpu.CompilerParams(
            collective_id=0, has_side_effects=True, vmem_limit_bytes=58 * 1024 * 1024
        ),
    )(queries, key_states, value_states, grad_out, tile_mask, block_order)
    return pl.pallas_call(
        write_out,
        out_shape=shapes,
        in_specs=[vmem] * 4,
        out_specs=(hbm,) * 4,
        scratch_shapes=[dma((4,))],
        compiler_params=pltpu.CompilerParams(vmem_limit_bytes=8 * 1024 * 1024),
    )(*results)


def solution(mesh):
    both = P(("groups", "blk"), None)
    return jax.shard_map(
        shards,
        mesh=mesh,
        in_specs=(both, both, both, both, P("groups", None), P("groups")),
        out_specs=(both, both, both, both),
        check_vma=False,
    )
```

time: 32.7 us -> 27.7 us (0.85)
  Pallas kernels: 32 us -> 26.9 us
    pallas_call x1, Pallas kernels: 31.2 us -> 26.1 us  [shards(): pl.pallas_call(functools.partial(kernel, n), out_shape=tuple((pltpu.VMEM(...]
where the time goes in v1:
time: 27.7 us; the launch traced here: 27.5 us
  Pallas kernels  26.9 us (97%)
  between operations  0.64 us (2%)
    pallas_call x1, Pallas kernels, shards(): pl.pallas_call(functools.partial(kernel, n), out_shape=tuple((pltpu.VMEM(...  26.1 us
    pallas_call x1, Pallas kernels, shards(): pl.pallas_call(write_out, out_shape=shapes, in_specs=[vmem] * 4, out_spec...  0.77 us

profile of v1, /device:TPU:0, one launch (start us, length us, event | category | flops | bytes accessed | tf_op | source)
XLA Modules:
  0.0 27.5 jit_solution(9803024046340560169)
XLA Ops:
  0.6 26.1 %shard_map.93 = (bf16[128,512]{1,0:T(8,128)(2,1)S(1)}, bf16[128,512]{1,0:T(8,128)(2,1)S(1)}, f32[128,128]{1,0:T(8,128)S(1)}, f32[128,128]{1,0:T(8,128)S(1)}) custom-call(bf16[128,512]{1,0:T(8,128)(2,1)} %q_hbm.1, bf16[128,128]{1,0:T(8,128)(2,1)} %k_hbm.1, bf16[128,128]{1,0:T(8,128)(2,1)} %v_hbm.1, bf16[128,512]{1,0:T(8,128)(2,1)} %g_hbm.1, ...), custom_call_target="tpu_custom_call" | custom-call | tf_op jit(solution)/shard_map/pallas_call | solution.py:299
  26.8 0.8 %shard_map.94 = (bf16[128,512]{1,0:T(8,128)(2,1)}, bf16[128,512]{1,0:T(8,128)(2,1)}, f32[128,128]{1,0:T(8,128)}, f32[128,128]{1,0:T(8,128)}) custom-call(bf16[128,512]{1,0:T(8,128)(2,1)S(1)} %get-tuple-element.8.refs_0_, bf16[128,512]{1,0:T(8,128)(2,1)S(1)} %get-tuple-element.9.refs_1_, f32[128,128]{1,0:T(8,128)S(1)} %get-tuple-element.10.refs_2_, ...), custom_call_target="tpu_custom_call" | custom-call | tf_op jit(solution)/shard_map/pallas_call | solution.py:328

commit v2 on v1

--- a/solution.py
+++ b/solution.py
@@ -24,7 +24,7 @@
 
 def kernel(
     n, q_hbm, k_hbm, v_hbm, g_hbm, mask_hbm, order_hbm, att_ref, dq_ref, dk_ref, dv_ref,
-    mask_ref, order_ref, q_ref, g_ref, kv, rt, prob, dprob, stat, mine, send_z, recv_z, send_c, recv_c, send_y, recv_y,
+    mask_ref, order_ref, q_ref, g_ref, kv, rt, prob, prod, left, raw, stat, mine, send_z, recv_z, send_c, recv_c, send_y, recv_y,
     in_s, z_s, z_r, y_s, y_r, c_s, c_r, f_s, f_r, t_s, t_r, gz_s, gz_r, gc_s, gc_r, gy_s, gy_r,
 ):
     m = n // 4
@@ -163,15 +163,19 @@
         share(0, j).start()
 
     def prob_grad(j):
-        total = jnp.zeros((1, rows), F32)
         grads = dot(flat(VALUE), rt[GRAD, j])
-        dprob[j] = grads
-        mine[1, j] = jnp.sum(prob[j].astype(F32) * grads, axis=0, keepdims=True)
+        grads = prob[j].astype(F32) * grads
+        mine[1, j] = jnp.sum(grads, axis=0, keepdims=True)
+        prod[j] = grads.astype(BF16)
+        raw[j, :2 * hd] = dot(left[...], prob[j])
+        raw[j, 2 * hd:] = dot(left[hd:], prod[j])
 
     gather_y(GRAD).wait_recv()
     forward(GRAD).start()
     for rz in range(1, m):
         gather_z(VALUE, rz).wait_recv()
+    left[:hd] = flat(VALUE).T
+    left[hd:] = flat(KEY).T
     prob_grad(OWN)
     gather_c(GRAD).wait_recv()
     prob_grad(SIBLING)
@@ -195,11 +199,10 @@
     for j in others:
         share(1, j).start()
 
-    def key_side(t):
+    def key_side(weights, sides):
         total = jnp.zeros((keys, hd), F32)
         for j in quad:
-            scaled = (rt[t, j].astype(F32) * factors[j]).astype(BF16)
-            total = total + dot_t(prob[j], scaled)
+            total = total + dot_t(weights[j], sides[j])
         return total
 
     def send_key_side(t, total):
@@ -208,21 +211,23 @@
             sum_z(t, rz).start()
         return total[:tok]
 
-    def query_side(t, left, j, by):
-        return dot(left, prob[j]) * (factors[j] * by)
-
-    def start_query_side(t, left, by):
-        send_c[t, 0] = query_side(t, left, DIAGONAL, by).astype(BF16)
+    def start_query_side(t, part):
+        send_c[t, 0] = part(DIAGONAL).astype(BF16)
         sum_c(t, 0).start()
-        return query_side(t, left, PARTNER, by)
-
-    def end_query_side(t, left, by, part):
+
+    def pass_query_side(t, part):
+        total = part(PARTNER)
         sum_c(t, 0).wait_recv()
-        send_y[t] = (part + recv_c[t, 0].astype(F32)).astype(BF16)
+        send_y[t] = (total + recv_c[t, 0].astype(F32)).astype(BF16)
         sum_y(t).start()
-        send_c[t, 1] = query_side(t, left, SIBLING, by).astype(BF16)
+        send_c[t, 1] = part(SIBLING).astype(BF16)
         sum_c(t, 1).start()
-        return query_side(t, left, OWN, by)
+
+    def out_part(j):
+        return raw[j, :hd] * factors[j]
+
+    def dq_part(j):
+        return (raw[j, 2 * hd:] - raw[j, hd:2 * hd] * deltas[j]) * (factors[j] * scale)
 
     def finish_query_side(t, total, out_ref):
         sum_c(t, 1).wait_recv()
@@ -238,25 +243,25 @@
             total = total + recv_z[t, m - rz].astype(F32)
         out_ref[...] = total * by
 
-    dv = send_key_side(VALUE, key_side(VALUE))
-    values_t = flat(VALUE).T
-    out_part = start_query_side(OUT, values_t, 1.0)
-    out = end_query_side(OUT, values_t, 1.0, out_part)
+    start_query_side(OUT, out_part)
+    scaled = [(rt[GRAD, j].astype(F32) * factors[j]).astype(BF16) for j in quad]
+    dv = send_key_side(VALUE, key_side(prob, scaled))
+    pass_query_side(OUT, out_part)
+    scaled = [rt[QUERY, j].astype(F32) * factors[j] for j in quad]
+    first = key_side(prod, [side.astype(BF16) for side in scaled])
 
     for j in others:
         share(1, j).wait_recv()
-    for j in (DIAGONAL, PARTNER, SIBLING, OWN):
-        delta = sum(shared(1, r, j) for r in quad)
-        prob[j] = (prob[j].astype(F32) * (dprob[j] - delta)).astype(BF16)
-    keys_t = flat(KEY).T
-    dq_part = start_query_side(DQ, keys_t, scale)
-    dk = send_key_side(KEY, key_side(KEY))
-    dq = end_query_side(DQ, keys_t, scale, dq_part)
-
-    finish_query_side(OUT, out, att_ref)
+    deltas = [sum(shared(1, r, j) for r in quad) for j in quad]
+    start_query_side(DQ, dq_part)
+    dk = first - key_side(prob, [(side * delta).astype(BF16) for side, delta in zip(scaled, deltas)])
+    dk = send_key_side(KEY, dk)
+    pass_query_side(DQ, dq_part)
+
+    finish_query_side(OUT, out_part(OWN), att_ref)
     finish_key_side(VALUE, dv, dv_ref, 1.0)
     finish_key_side(KEY, dk, dk_ref, scale)
-    finish_query_side(DQ, dq, dq_ref)
+    finish_query_side(DQ, dq_part(OWN), dq_ref)
 
     for t in (0, 1):
         gather_y(t).wait_send()
@@ -309,7 +314,9 @@
             pltpu.VMEM((2, m, tok, hd), BF16),
             pltpu.VMEM((2, 4, hd, rows), BF16),
             pltpu.VMEM((4, m * tok, rows), BF16),
-            pltpu.VMEM((4, m * tok, rows), F32),
+            pltpu.VMEM((4, m * tok, rows), BF16),
+            pltpu.VMEM((2 * hd, m * tok), BF16),
+            pltpu.VMEM((4, 3 * hd, rows), F32),
             pltpu.VMEM((2, 4, 1, 4 * rows), F32),
             pltpu.VMEM((2, 4, 1, rows), F32),
             pltpu.VMEM((2, m, tok, hd), BF16),

time: 27.7 us -> 27.1 us (0.978)
  Pallas kernels: 26.9 us -> 26.3 us
    pallas_call x1, Pallas kernels: 26.1 us -> 25.5 us  [shards(): pl.pallas_call(functools.partial(kernel, n), out_shape=tuple((pltpu.VMEM(...]
where the time goes in v2:
time: 27.1 us; the launch traced here: 26.9 us
  Pallas kernels  26.3 us (97%)
  between operations  0.64 us (2%)
    pallas_call x1, Pallas kernels, shards(): pl.pallas_call(functools.partial(kernel, n), out_shape=tuple((pltpu.VMEM(...  25.5 us
    pallas_call x1, Pallas kernels, shards(): pl.pallas_call(write_out, out_shape=shapes, in_specs=[vmem] * 4, out_spec...  0.77 us

profile of v2, /device:TPU:0, one launch (start us, length us, event | category | flops | bytes accessed | tf_op | source)
XLA Modules:
  0.0 26.9 jit_solution(16620485206782201016)
XLA Ops:
  0.6 25.5 %shard_map.93 = (bf16[128,512]{1,0:T(8,128)(2,1)S(1)}, bf16[128,512]{1,0:T(8,128)(2,1)S(1)}, f32[128,128]{1,0:T(8,128)S(1)}, f32[128,128]{1,0:T(8,128)S(1)}) custom-call(bf16[128,512]{1,0:T(8,128)(2,1)} %q_hbm.1, bf16[128,128]{1,0:T(8,128)(2,1)} %k_hbm.1, bf16[128,128]{1,0:T(8,128)(2,1)} %v_hbm.1, bf16[128,512]{1,0:T(8,128)(2,1)} %g_hbm.1, ...), custom_call_target="tpu_custom_call" | custom-call | tf_op jit(solution)/shard_map/pallas_call | solution.py:304
  26.2 0.8 %shard_map.94 = (bf16[128,512]{1,0:T(8,128)(2,1)}, bf16[128,512]{1,0:T(8,128)(2,1)}, f32[128,128]{1,0:T(8,128)}, f32[128,128]{1,0:T(8,128)}) custom-call(bf16[128,512]{1,0:T(8,128)(2,1)S(1)} %get-tuple-element.8.refs_0_, bf16[128,512]{1,0:T(8,128)(2,1)S(1)} %get-tuple-element.9.refs_1_, f32[128,128]{1,0:T(8,128)S(1)} %get-tuple-element.10.refs_2_, ...), custom_call_target="tpu_custom_call" | custom-call | tf_op jit(solution)/shard_map/pallas_call | solution.py:335

commit v3 on v2

--- a/solution.py
+++ b/solution.py
@@ -78,7 +78,8 @@
         return remote(send_z.at[t, rz], recv_z.at[t, m - rz], gz_s.at[t, rz], gz_r.at[t, m - rz], chunk(rz))
 
     def sum_c(t, i):
-        return remote(send_c.at[t, i], recv_c.at[t, i], gc_s.at[t, i], gc_r.at[t, i], index(0, SIBLING))
+        part = pl.ds(2 * hd, hd) if t else pl.ds(0, 2 * hd)
+        return remote(send_c.at[i, part], recv_c.at[i, part], gc_s.at[t, i], gc_r.at[t, i], index(0, SIBLING))
 
     def sum_y(t):
         return remote(send_y.at[t], recv_y.at[t], gy_s.at[t], gy_r.at[t], index(0, PARTNER))
@@ -105,9 +106,9 @@
 
     far = sorted(range(1, m), key=lambda r: -min(r, m - r))
     for t in (0, 1):
+        gather_y(t).start()
         for rz in far:
             gather_z(t, rz).start()
-        gather_y(t).start()
         gather_c(t).start()
 
     blocks = [order_ref[index(0, j)] for j in quad]
@@ -146,8 +147,10 @@
                 p = jnp.exp2(s * to_exp2 + (b - top))
             total = total + jnp.sum(p, axis=0, keepdims=True)
             prob[j, rz * tok:(rz + 1) * tok, :] = p.astype(BF16)
+        log_sum = top + jnp.log2(jnp.maximum(total, 1e-37))
         mine[0, j] = top
-        stat[0, OWN, :, j * rows:(j + 1) * rows] = top + jnp.log2(jnp.maximum(total, 1e-37))
+        mine[1, j] = jnp.exp2(top - log_sum)
+        stat[0, OWN, :, j * rows:(j + 1) * rows] = log_sum
 
     gather_y(QUERY).wait_recv()
     forward(QUERY).start()
@@ -162,13 +165,20 @@
     for j in others:
         share(0, j).start()
 
+    def query_side(j, t):
+        part = slice(2 * hd, 3 * hd) if t else slice(0, 2 * hd)
+        product = dot(left[hd:], prod[j]) if t else dot(left[...], prob[j])
+        if j & 1 == j >> 1:
+            raw[0 if j else 1, part] = product
+        else:
+            i = 0 if j == DIAGONAL else 1
+            send_c[i, part] = (product * mine[1, j]).astype(BF16)
+            sum_c(t, i).start()
+
     def prob_grad(j):
-        grads = dot(flat(VALUE), rt[GRAD, j])
-        grads = prob[j].astype(F32) * grads
-        mine[1, j] = jnp.sum(grads, axis=0, keepdims=True)
+        grads = prob[j].astype(F32) * dot(flat(VALUE), rt[GRAD, j])
         prod[j] = grads.astype(BF16)
-        raw[j, :2 * hd] = dot(left[...], prob[j])
-        raw[j, 2 * hd:] = dot(left[hd:], prod[j])
+        stat[1, OWN, :, j * rows:(j + 1) * rows] = jnp.sum(grads, axis=0, keepdims=True) * mine[1, j]
 
     gather_y(GRAD).wait_recv()
     forward(GRAD).start()
@@ -176,28 +186,31 @@
         gather_z(VALUE, rz).wait_recv()
     left[:hd] = flat(VALUE).T
     left[hd:] = flat(KEY).T
+    for j in (DIAGONAL, SIBLING, PARTNER, OWN):
+        query_side(j, 0)
     prob_grad(OWN)
     gather_c(GRAD).wait_recv()
     prob_grad(SIBLING)
     prob_grad(PARTNER)
     forward(GRAD).wait_recv()
     prob_grad(DIAGONAL)
+    for j in others:
+        share(1, j).start()
+    for j in (DIAGONAL, SIBLING, PARTNER, OWN):
+        query_side(j, 1)
 
     def shared(t, r, j):
         return stat[t, r, :, (r ^ j) * rows:((r ^ j) + 1) * rows]
 
     for j in others:
         share(0, j).wait_recv()
-    factors = []
+    shares, factors = [], []
     for j in quad:
         parts = [shared(0, r, j) for r in quad]
         top = jnp.maximum(jnp.maximum(parts[0], parts[1]), jnp.maximum(parts[2], parts[3]))
-        total = sum(jnp.exp2(part - top) for part in parts)
-        factor = jnp.exp2(mine[0, j] - top - jnp.log2(total))
-        factors.append(factor)
-        stat[1, OWN, :, j * rows:(j + 1) * rows] = mine[1, j] * factor
-    for j in others:
-        share(1, j).start()
+        log_sum = top + jnp.log2(sum(jnp.exp2(part - top) for part in parts))
+        shares.append([jnp.exp2(part - log_sum) for part in parts])
+        factors.append(jnp.exp2(mine[0, j] - log_sum))
 
     def key_side(weights, sides):
         total = jnp.zeros((keys, hd), F32)
@@ -211,27 +224,23 @@
             sum_z(t, rz).start()
         return total[:tok]
 
-    def start_query_side(t, part):
-        send_c[t, 0] = part(DIAGONAL).astype(BF16)
-        sum_c(t, 0).start()
+    def both_cores(i, t):
+        j = OWN if i else PARTNER
+        part = slice(t * hd, (t + 1) * hd)
+        return raw[i, part] * factors[j] + recv_c[i, part].astype(F32) * shares[j][SIBLING]
+
+    def out_part(i):
+        return both_cores(i, 0)
+
+    def dq_part(i):
+        return (both_cores(i, 2) - both_cores(i, 1) * deltas[OWN if i else PARTNER]) * scale
 
     def pass_query_side(t, part):
-        total = part(PARTNER)
         sum_c(t, 0).wait_recv()
-        send_y[t] = (total + recv_c[t, 0].astype(F32)).astype(BF16)
+        send_y[t] = part(0).astype(BF16)
         sum_y(t).start()
-        send_c[t, 1] = part(SIBLING).astype(BF16)
-        sum_c(t, 1).start()
-
-    def out_part(j):
-        return raw[j, :hd] * factors[j]
-
-    def dq_part(j):
-        return (raw[j, 2 * hd:] - raw[j, hd:2 * hd] * deltas[j]) * (factors[j] * scale)
 
     def finish_query_side(t, total, out_ref):
-        sum_c(t, 1).wait_recv()
-        total = total + recv_c[t, 1].astype(F32)
         sum_y(t).wait_recv()
         total = (total + recv_y[t].astype(F32)).astype(BF16)
         for h in range(heads):
@@ -243,25 +252,25 @@
             total = total + recv_z[t, m - rz].astype(F32)
         out_ref[...] = total * by
 
-    start_query_side(OUT, out_part)
+    pass_query_side(OUT, out_part)
     scaled = [(rt[GRAD, j].astype(F32) * factors[j]).astype(BF16) for j in quad]
     dv = send_key_side(VALUE, key_side(prob, scaled))
-    pass_query_side(OUT, out_part)
     scaled = [rt[QUERY, j].astype(F32) * factors[j] for j in quad]
     first = key_side(prod, [side.astype(BF16) for side in scaled])
 
     for j in others:
         share(1, j).wait_recv()
-    deltas = [sum(shared(1, r, j) for r in quad) for j in quad]
-    start_query_side(DQ, dq_part)
+    deltas = [sum(shared(1, r, j) * shares[j][r] for r in quad) for j in quad]
+    pass_query_side(DQ, dq_part)
     dk = first - key_side(prob, [(side * delta).astype(BF16) for side, delta in zip(scaled, deltas)])
     dk = send_key_side(KEY, dk)
-    pass_query_side(DQ, dq_part)
-
-    finish_query_side(OUT, out_part(OWN), att_ref)
+
+    sum_c(OUT, 1).wait_recv()
+    finish_query_side(OUT, out_part(1), att_ref)
     finish_key_side(VALUE, dv, dv_ref, 1.0)
     finish_key_side(KEY, dk, dk_ref, scale)
-    finish_query_side(DQ, dq_part(OWN), dq_ref)
+    sum_c(DQ, 1).wait_recv()
+    finish_query_side(DQ, dq_part(1), dq_ref)
 
     for t in (0, 1):
         gather_y(t).wait_send()
@@ -316,13 +325,13 @@
             pltpu.VMEM((4, m * tok, rows), BF16),
             pltpu.VMEM((4, m * tok, rows), BF16),
             pltpu.VMEM((2 * hd, m * tok), BF16),
-            pltpu.VMEM((4, 3 * hd, rows), F32),
+            pltpu.VMEM((2, 3 * hd, rows), F32),
             pltpu.VMEM((2, 4, 1, 4 * rows), F32),
             pltpu.VMEM((2, 4, 1, rows), F32),
             pltpu.VMEM((2, m, tok, hd), BF16),
             pltpu.VMEM((2, m, tok, hd), BF16),
-            pltpu.VMEM((2, 2, hd, rows), BF16),
-            pltpu.VMEM((2, 2, hd, rows), BF16),
+            pltpu.VMEM((2, 3 * hd, rows), BF16),
+            pltpu.VMEM((2, 3 * hd, rows), BF16),
             pltpu.VMEM((2, hd, rows), BF16),
             pltpu.VMEM((2, hd, rows), BF16),
             dma((6,)), dma((2, m)), dma((2, m)), dma((2,)), dma((2,)), dma((2,)), dma((2,)), dma((2,)), dma((2,)),

time: 27.1 us -> 26 us (0.959)
  Pallas kernels: 26.3 us -> 25.2 us
    pallas_call x1, Pallas kernels: 25.5 us -> 24.4 us  [shards(): pl.pallas_call(functools.partial(kernel, n), out_shape=tuple((pltpu.VMEM(...]
where the time goes in v3:
time: 26 us; the launch traced here: 25.9 us
  Pallas kernels  25.2 us (97%)
  between operations  0.64 us (2%)
    pallas_call x1, Pallas kernels, shards(): pl.pallas_call(functools.partial(kernel, n), out_shape=tuple((pltpu.VMEM(...  24.4 us
    pallas_call x1, Pallas kernels, shards(): pl.pallas_call(write_out, out_shape=shapes, in_specs=[vmem] * 4, out_spec...  0.77 us

profile of v3, /device:TPU:0, one launch (start us, length us, event | category | flops | bytes accessed | tf_op | source)
XLA Modules:
  0.0 25.9 jit_solution(3175478306942788214)
XLA Ops:
  0.6 24.4 %shard_map.93 = (bf16[128,512]{1,0:T(8,128)(2,1)S(1)}, bf16[128,512]{1,0:T(8,128)(2,1)S(1)}, f32[128,128]{1,0:T(8,128)S(1)}, f32[128,128]{1,0:T(8,128)S(1)}) custom-call(bf16[128,512]{1,0:T(8,128)(2,1)} %q_hbm.1, bf16[128,128]{1,0:T(8,128)(2,1)} %k_hbm.1, bf16[128,128]{1,0:T(8,128)(2,1)} %v_hbm.1, bf16[128,512]{1,0:T(8,128)(2,1)} %g_hbm.1, ...), custom_call_target="tpu_custom_call" | custom-call | tf_op jit(solution)/shard_map/pallas_call | solution.py:313
  25.1 0.8 %shard_map.94 = (bf16[128,512]{1,0:T(8,128)(2,1)}, bf16[128,512]{1,0:T(8,128)(2,1)}, f32[128,128]{1,0:T(8,128)}, f32[128,128]{1,0:T(8,128)}) custom-call(bf16[128,512]{1,0:T(8,128)(2,1)S(1)} %get-tuple-element.8.refs_0_, bf16[128,512]{1,0:T(8,128)(2,1)S(1)} %get-tuple-element.9.refs_1_, f32[128,128]{1,0:T(8,128)S(1)} %get-tuple-element.10.refs_2_, ...), custom_call_target="tpu_custom_call" | custom-call | tf_op jit(solution)/shard_map/pallas_call | solution.py:344

commit v4 on v3

--- a/solution.py
+++ b/solution.py
@@ -65,8 +65,8 @@
     def gather_y(t):
         return remote(rt.at[t, OWN], rt.at[t, PARTNER], y_s.at[t], y_r.at[t], index(0, PARTNER))
 
-    def gather_c(t):
-        return remote(rt.at[t, OWN], rt.at[t, SIBLING], c_s.at[t], c_r.at[t], index(0, SIBLING))
+    def gather_c():
+        return remote(rt.at[:, OWN], rt.at[:, SIBLING], c_s.at[0], c_r.at[0], index(0, SIBLING))
 
     def forward(t):
         return remote(rt.at[t, PARTNER], rt.at[t, DIAGONAL], f_s.at[t], f_r.at[t], index(0, SIBLING))
@@ -109,7 +109,8 @@
         gather_y(t).start()
         for rz in far:
             gather_z(t, rz).start()
-        gather_c(t).start()
+        if t == 0:
+            gather_c().start()
 
     blocks = [order_ref[index(0, j)] for j in quad]
     key_ids = lax.broadcasted_iota(jnp.int32, (tok, rows), 0)
@@ -157,13 +158,14 @@
     for rz in range(1, m):
         gather_z(KEY, rz).wait_recv()
     score(OWN)
-    gather_c(QUERY).wait_recv()
+    gather_c().wait_recv()
     score(SIBLING)
     score(PARTNER)
     forward(QUERY).wait_recv()
     score(DIAGONAL)
     for j in others:
         share(0, j).start()
+    left[hd:] = flat(KEY).T
 
     def query_side(j, t):
         part = slice(2 * hd, 3 * hd) if t else slice(0, 2 * hd)
@@ -184,20 +186,18 @@
     forward(GRAD).start()
     for rz in range(1, m):
         gather_z(VALUE, rz).wait_recv()
-    left[:hd] = flat(VALUE).T
-    left[hd:] = flat(KEY).T
-    for j in (DIAGONAL, SIBLING, PARTNER, OWN):
-        query_side(j, 0)
     prob_grad(OWN)
-    gather_c(GRAD).wait_recv()
     prob_grad(SIBLING)
     prob_grad(PARTNER)
+    left[:hd] = flat(VALUE).T
+    query_side(DIAGONAL, 0)
     forward(GRAD).wait_recv()
     prob_grad(DIAGONAL)
     for j in others:
         share(1, j).start()
-    for j in (DIAGONAL, SIBLING, PARTNER, OWN):
-        query_side(j, 1)
+    query_side(DIAGONAL, 1)
+    query_side(PARTNER, 0)
+    query_side(PARTNER, 1)
 
     def shared(t, r, j):
         return stat[t, r, :, (r ^ j) * rows:((r ^ j) + 1) * rows]
@@ -212,16 +212,16 @@
         shares.append([jnp.exp2(part - log_sum) for part in parts])
         factors.append(jnp.exp2(mine[0, j] - log_sum))
 
-    def key_side(weights, sides):
-        total = jnp.zeros((keys, hd), F32)
-        for j in quad:
-            total = total + dot_t(weights[j], sides[j])
-        return total
-
-    def send_key_side(t, total):
-        for rz in far:
-            send_z[t, rz] = total[rz * tok:(rz + 1) * tok].astype(BF16)
-            sum_z(t, rz).start()
+    def key_side(weights, sides, start, stop):
+        return sum(dot_t(weights[j, start * tok:stop * tok], sides[j]) for j in quad)
+
+    def send_key_side(t, make):
+        for start, stop in ((m // 4, m - m // 4), (m - m // 4, m), (0, m // 4)):
+            total = make(start, stop)
+            for rz in sorted(range(start, stop), key=lambda r: -min(r, m - r)):
+                if rz:
+                    send_z[t, rz] = total[(rz - start) * tok:(rz - start + 1) * tok].astype(BF16)
+                    sum_z(t, rz).start()
         return total[:tok]
 
     def both_cores(i, t):
@@ -253,37 +253,48 @@
         out_ref[...] = total * by
 
     pass_query_side(OUT, out_part)
-    scaled = [(rt[GRAD, j].astype(F32) * factors[j]).astype(BF16) for j in quad]
-    dv = send_key_side(VALUE, key_side(prob, scaled))
+    scaled_grads = [(rt[GRAD, j].astype(F32) * factors[j]).astype(BF16) for j in quad]
+    dv = send_key_side(VALUE, lambda start, stop: key_side(prob, scaled_grads, start, stop))
+    query_side(SIBLING, 0)
+    query_side(SIBLING, 1)
+    query_side(OWN, 0)
+    query_side(OWN, 1)
     scaled = [rt[QUERY, j].astype(F32) * factors[j] for j in quad]
-    first = key_side(prod, [side.astype(BF16) for side in scaled])
+    first = key_side(prod, [side.astype(BF16) for side in scaled], 0, m)
 
     for j in others:
         share(1, j).wait_recv()
     deltas = [sum(shared(1, r, j) * shares[j][r] for r in quad) for j in quad]
     pass_query_side(DQ, dq_part)
-    dk = first - key_side(prob, [(side * delta).astype(BF16) for side, delta in zip(scaled, deltas)])
-    dk = send_key_side(KEY, dk)
-
-    sum_c(OUT, 1).wait_recv()
-    finish_query_side(OUT, out_part(1), att_ref)
-    finish_key_side(VALUE, dv, dv_ref, 1.0)
-    finish_key_side(KEY, dk, dk_ref, scale)
-    sum_c(DQ, 1).wait_recv()
-    finish_query_side(DQ, dq_part(1), dq_ref)
+    lowered = [(side * delta).astype(BF16) for side, delta in zip(scaled, deltas)]
+    dk = send_key_side(
+        KEY, lambda start, stop: first[start * tok:stop * tok] - key_side(prob, lowered, start, stop)
+    )
 
     for t in (0, 1):
         gather_y(t).wait_send()
-        gather_c(t).wait_send()
+        if t == 0:
+            gather_c().wait_send()
         forward(t).wait_send()
-        sum_y(t).wait_send()
         for i in (0, 1):
             sum_c(t, i).wait_send()
         for j in others:
             share(t, j).wait_send()
         for rz in range(1, m):
             gather_z(t, rz).wait_send()
-            sum_z(t, rz).wait_send()
+    sum_c(OUT, 1).wait_recv()
+    finish_query_side(OUT, out_part(1), att_ref)
+    finish_key_side(VALUE, dv, dv_ref, 1.0)
+    sum_y(OUT).wait_send()
+    for rz in far:
+        sum_z(VALUE, rz).wait_send()
+    sum_c(DQ, 1).wait_recv()
+    dq = dq_part(1)
+    for rz in far:
+        sum_z(KEY, rz).wait_send()
+    sum_y(DQ).wait_send()
+    finish_key_side(KEY, dk, dk_ref, scale)
+    finish_query_side(DQ, dq, dq_ref)
 
 
 def write_out(*refs):

time: 26 us -> 24.6 us (0.946)
  Pallas kernels: 25.2 us -> 23.8 us
    pallas_call x1, Pallas kernels: 24.4 us -> 23 us  [shards(): pl.pallas_call(functools.partial(kernel, n), out_shape=tuple((pltpu.VMEM(...]
where the time goes in v4:
time: 24.6 us; the launch traced here: 24.4 us
  Pallas kernels  23.8 us (97%)
  between operations  0.64 us (3%)
    pallas_call x1, Pallas kernels, shards(): pl.pallas_call(functools.partial(kernel, n), out_shape=tuple((pltpu.VMEM(...  23 us
    pallas_call x1, Pallas kernels, shards(): pl.pallas_call(write_out, out_shape=shapes, in_specs=[vmem] * 4, out_spec...  0.77 us

profile of v4, /device:TPU:0, one launch (start us, length us, event | category | flops | bytes accessed | tf_op | source)
XLA Modules:
  0.0 24.4 jit_solution(12700806326113220294)
XLA Ops:
  0.6 23.0 %shard_map.93 = (bf16[128,512]{1,0:T(8,128)(2,1)S(1)}, bf16[128,512]{1,0:T(8,128)(2,1)S(1)}, f32[128,128]{1,0:T(8,128)S(1)}, f32[128,128]{1,0:T(8,128)S(1)}) custom-call(bf16[128,512]{1,0:T(8,128)(2,1)} %q_hbm.1, bf16[128,128]{1,0:T(8,128)(2,1)} %k_hbm.1, bf16[128,128]{1,0:T(8,128)(2,1)} %v_hbm.1, bf16[128,512]{1,0:T(8,128)(2,1)} %g_hbm.1, ...), custom_call_target="tpu_custom_call" | custom-call | tf_op jit(solution)/shard_map/pallas_call | solution.py:324
  23.6 0.8 %shard_map.94 = (bf16[128,512]{1,0:T(8,128)(2,1)}, bf16[128,512]{1,0:T(8,128)(2,1)}, f32[128,128]{1,0:T(8,128)}, f32[128,128]{1,0:T(8,128)}) custom-call(bf16[128,512]{1,0:T(8,128)(2,1)S(1)} %get-tuple-element.8.refs_0_, bf16[128,512]{1,0:T(8,128)(2,1)S(1)} %get-tuple-element.9.refs_1_, f32[128,128]{1,0:T(8,128)S(1)} %get-tuple-element.10.refs_2_, ...), custom_call_target="tpu_custom_call" | custom-call | tf_op jit(solution)/shard_map/pallas_call | solution.py:355

commit v5 on v4

--- a/solution.py
+++ b/solution.py
@@ -96,21 +96,24 @@
     ]
     for load in loads:
         load.start()
-    for t, ref in ((QUERY, q_ref), (GRAD, g_ref)):
+    far = sorted(range(1, m), key=lambda r: -min(r, m - r))
+    def turn(t, ref):
         loads[t].wait()
         for h in range(heads):
             rt[t, OWN, :, h * tok:(h + 1) * tok] = ref[:, h * hd:(h + 1) * hd].T
+
+    turn(QUERY, q_ref)
+    turn(GRAD, g_ref)
     for load in loads[2:]:
         load.wait()
     pl.semaphore_wait(barrier, m + 2)
-
-    far = sorted(range(1, m), key=lambda r: -min(r, m - r))
-    for t in (0, 1):
-        gather_y(t).start()
-        for rz in far:
-            gather_z(t, rz).start()
-        if t == 0:
-            gather_c().start()
+    gather_y(QUERY).start()
+    for rz in far:
+        gather_z(KEY, rz).start()
+    gather_y(GRAD).start()
+    gather_c().start()
+    for rz in far:
+        gather_z(VALUE, rz).start()
 
     blocks = [order_ref[index(0, j)] for j in quad]
     key_ids = lax.broadcasted_iota(jnp.int32, (tok, rows), 0)
@@ -216,7 +219,7 @@
         return sum(dot_t(weights[j, start * tok:stop * tok], sides[j]) for j in quad)
 
     def send_key_side(t, make):
-        for start, stop in ((m // 4, m - m // 4), (m - m // 4, m), (0, m // 4)):
+        for start, stop in [(rz, rz + 1) for rz in far + [0]]:
             total = make(start, stop)
             for rz in sorted(range(start, stop), key=lambda r: -min(r, m - r)):
                 if rz:
@@ -290,11 +293,11 @@
         sum_z(VALUE, rz).wait_send()
     sum_c(DQ, 1).wait_recv()
     dq = dq_part(1)
+    finish_query_side(DQ, dq, dq_ref)
+    finish_key_side(KEY, dk, dk_ref, scale)
     for rz in far:
         sum_z(KEY, rz).wait_send()
     sum_y(DQ).wait_send()
-    finish_key_side(KEY, dk, dk_ref, scale)
-    finish_query_side(DQ, dq, dq_ref)
 
 
 def write_out(*refs):

time: 24.6 us -> 24.5 us (level)
  no operation moved by 1% of the time
where the time goes in v5:
time: 24.5 us; the launch traced here: 24.4 us
  Pallas kernels  23.7 us (97%)
  between operations  0.64 us (3%)
    pallas_call x1, Pallas kernels, shards(): pl.pallas_call(functools.partial(kernel, n), out_shape=tuple((pltpu.VMEM(...  22.9 us
    pallas_call x1, Pallas kernels, shards(): pl.pallas_call(write_out, out_shape=shapes, in_specs=[vmem] * 4, out_spec...  0.77 us

profile of v5, /device:TPU:0, one launch (start us, length us, event | category | flops | bytes accessed | tf_op | source)
XLA Modules:
  0.0 24.4 jit_solution(4821672392658422408)
XLA Ops:
  0.6 22.9 %shard_map.93 = (bf16[128,512]{1,0:T(8,128)(2,1)S(1)}, bf16[128,512]{1,0:T(8,128)(2,1)S(1)}, f32[128,128]{1,0:T(8,128)S(1)}, f32[128,128]{1,0:T(8,128)S(1)}) custom-call(bf16[128,512]{1,0:T(8,128)(2,1)} %q_hbm.1, bf16[128,128]{1,0:T(8,128)(2,1)} %k_hbm.1, bf16[128,128]{1,0:T(8,128)(2,1)} %v_hbm.1, bf16[128,512]{1,0:T(8,128)(2,1)} %g_hbm.1, ...), custom_call_target="tpu_custom_call" | custom-call | tf_op jit(solution)/shard_map/pallas_call | solution.py:327
  23.6 0.8 %shard_map.94 = (bf16[128,512]{1,0:T(8,128)(2,1)}, bf16[128,512]{1,0:T(8,128)(2,1)}, f32[128,128]{1,0:T(8,128)}, f32[128,128]{1,0:T(8,128)}) custom-call(bf16[128,512]{1,0:T(8,128)(2,1)S(1)} %get-tuple-element.8.refs_0_, bf16[128,512]{1,0:T(8,128)(2,1)S(1)} %get-tuple-element.9.refs_1_, f32[128,128]{1,0:T(8,128)S(1)} %get-tuple-element.10.refs_2_, ...), custom_call_target="tpu_custom_call" | custom-call | tf_op jit(solution)/shard_map/pallas_call | solution.py:358

commit v6 on v5

--- a/solution.py
+++ b/solution.py
@@ -39,7 +39,7 @@
     OUT, DQ = 0, 1
     OWN, SIBLING, DIAGONAL, PARTNER = 0, 1, 2, 3
     quad = (OWN, SIBLING, DIAGONAL, PARTNER)
-    others = (DIAGONAL, PARTNER, SIBLING)
+    others = (PARTNER, SIBLING, DIAGONAL)
 
     me = lax.axis_index("blk")
     z, y, c = me // 4, (me // 2) % 2, me % 2

time: 24.5 us -> 24.2 us (0.988)
    pallas_call x1, Pallas kernels: 22.9 us -> 22.7 us  [shards(): pl.pallas_call(functools.partial(kernel, n), out_shape=tuple((pltpu.VMEM(...]
where the time goes in v6:
time: 24.2 us; the launch traced here: 24.1 us
  Pallas kernels  23.5 us (97%)
  between operations  0.64 us (3%)
    pallas_call x1, Pallas kernels, shards(): pl.pallas_call(functools.partial(kernel, n), out_shape=tuple((pltpu.VMEM(...  22.7 us
    pallas_call x1, Pallas kernels, shards(): pl.pallas_call(write_out, out_shape=shapes, in_specs=[vmem] * 4, out_spec...  0.77 us

profile of v6, /device:TPU:0, one launch (start us, length us, event | category | flops | bytes accessed | tf_op | source)
XLA Modules:
  0.0 24.1 jit_solution(5166155256975702819)
XLA Ops:
  0.6 22.7 %shard_map.93 = (bf16[128,512]{1,0:T(8,128)(2,1)S(1)}, bf16[128,512]{1,0:T(8,128)(2,1)S(1)}, f32[128,128]{1,0:T(8,128)S(1)}, f32[128,128]{1,0:T(8,128)S(1)}) custom-call(bf16[128,512]{1,0:T(8,128)(2,1)} %q_hbm.1, bf16[128,128]{1,0:T(8,128)(2,1)} %k_hbm.1, bf16[128,128]{1,0:T(8,128)(2,1)} %v_hbm.1, bf16[128,512]{1,0:T(8,128)(2,1)} %g_hbm.1, ...), custom_call_target="tpu_custom_call" | custom-call | tf_op jit(solution)/shard_map/pallas_call | solution.py:327
  23.3 0.8 %shard_map.94 = (bf16[128,512]{1,0:T(8,128)(2,1)}, bf16[128,512]{1,0:T(8,128)(2,1)}, f32[128,128]{1,0:T(8,128)}, f32[128,128]{1,0:T(8,128)}) custom-call(bf16[128,512]{1,0:T(8,128)(2,1)S(1)} %get-tuple-element.8.refs_0_, bf16[128,512]{1,0:T(8,128)(2,1)S(1)} %get-tuple-element.9.refs_1_, f32[128,128]{1,0:T(8,128)S(1)} %get-tuple-element.10.refs_2_, ...), custom_call_target="tpu_custom_call" | custom-call | tf_op jit(solution)/shard_map/pallas_call | solution.py:358
